TPU v7x, 32 devices: a whole 2x2x4 slice. The times are simulated.
32 devices in a mesh: dp: 8 (over z, x), mp: 4 (over y, core).
Axes of the slice: x: 2, y: 2, z: 4, core: 2. Of those that a mesh axis runs over, the one named last changes fastest.
Arguments:
- queries: bfloat16 [2048, 4096], P('dp', 'mp'), may hold values from -6 to 6
- keys: bfloat16 [2048, 4096], P('dp', 'mp'), may hold values from -6 to 6
- values: bfloat16 [2048, 4096], P('dp', 'mp'), may hold values from -12 to 12
- cotangent: bfloat16 [2048, 6144], P(('dp', 'mp')), may hold values from -0.796875 to 0.796875
- master: float32 [4096, 6144], P('mp', 'dp'), may hold values from -0.09375 to 0.09375
- moment_one: float32 [4096, 6144], P('mp', 'dp'), may hold values from -6 to 6
- moment_two: float32 [4096, 6144], P('mp', 'dp'), may hold values from 1 to 10
Outputs:
- attn_out: bfloat16 [2048, 6144], P(('dp', 'mp'))
- grad_queries: bfloat16 [2048, 4096], P('dp', 'mp')
- grad_keys: bfloat16 [2048, 4096], P('dp', 'mp')
- grad_values: bfloat16 [2048, 4096], P('dp', 'mp')
- new_master: float32 [4096, 6144], P('mp', 'dp')
- new_moment_one: float32 [4096, 6144], P('mp', 'dp')
- new_moment_two: float32 [4096, 6144], P('mp', 'dp')
All inputs are finite; a program needn't handle non-finite values.
Results may differ from a plain program's by a relative error of at most 0.014.
Values may be sent and summed in bfloat16 or wider, within the bound.
A program may use at most 128 MiB of HBM per device.

v0:
```python
import jax
import jax.numpy as jnp
from jax import lax
from jax.sharding import PartitionSpec as P

HEAD_DIM = 128
PATCHES = 256


def passed_along(block, axis, distance):
    devices = range(lax.axis_size(axis))
    route = [((i - distance) % len(devices), i) for i in devices]
    return lax.ppermute(block, axis, route)


def adam_update(grad_weight, master, moment_one, moment_two):
    new_one = 0.9 * moment_one + 0.1 * grad_weight
    new_two = 0.95 * moment_two + 0.05 * grad_weight * grad_weight
    new_master = master - 0.001 * (new_one / 0.19) / (jnp.sqrt(new_two / 0.0975) + 1e-08)
    return (new_master, new_one, new_two)


def local(queries, keys, values, cotangent, master, moment_one, moment_two):
    scaling = HEAD_DIM ** (-0.5)
    count_mp = lax.axis_size("mp")
    position = lax.axis_index("mp")
    rows_all = queries.shape[0]
    local_width = queries.shape[1]
    heads_here = local_width // HEAD_DIM
    images = rows_all // PATCHES
    span = cotangent.shape[0]
    shaped = (images, PATCHES, heads_here, HEAD_DIM)
    query_img = queries.reshape(shaped)
    key_img = keys.reshape(shaped)
    value_img = values.reshape(shaped)
    weight_full = lax.all_gather(master.astype(jnp.bfloat16), "dp", axis=1, tiled=True)
    scores = (
        jnp.einsum("iphd,iqhd->ihpq", query_img, key_img, preferred_element_type=jnp.float32)
        * scaling
    )
    probs = jax.nn.softmax(scores, axis=-1)
    probs_b = probs.astype(jnp.bfloat16)
    context = jnp.einsum("ihpq,iqhd->iphd", probs_b, value_img, preferred_element_type=jnp.float32)
    context = context.astype(jnp.bfloat16).reshape(rows_all, local_width)

    def partial_rows(block, columns):
        ctx_rows = lax.dynamic_slice_in_dim(context, block * span, span, 0)
        return jnp.dot(ctx_rows, columns, preferred_element_type=jnp.float32)

    def turn_one(turn, total):
        total = passed_along(total.astype(jnp.bfloat16), "mp", 1).astype(total.dtype)
        return total + partial_rows((position - turn - 1) % count_mp, weight_full)

    summed = lax.fori_loop(
        1, count_mp, turn_one, partial_rows((position - 1) % count_mp, weight_full)
    )
    attn_out = summed.astype(jnp.bfloat16)
    piece = lax.all_gather(cotangent, "mp", axis=0, tiled=True)
    ctx_rows = context
    grad_total = jnp.einsum("tk,td->kd", ctx_rows, piece, preferred_element_type=jnp.float32)
    dctx_rows = jnp.einsum(
        "td,kd->tk", piece, weight_full, preferred_element_type=jnp.float32
    ).astype(jnp.bfloat16)
    dctx_img = dctx_rows.reshape(shaped)
    grad_probs = jnp.einsum(
        "iphd,iqhd->ihpq", dctx_img, value_img, preferred_element_type=jnp.float32
    )
    inner = jnp.sum(probs * grad_probs, axis=-1, keepdims=True)
    grad_scores = (probs * (grad_probs - inner) * scaling).astype(jnp.bfloat16)
    grad_q = jnp.einsum("ihpq,iqhd->iphd", grad_scores, key_img, preferred_element_type=jnp.float32)
    grad_k = jnp.einsum(
        "ihpq,iphd->iqhd", grad_scores, query_img, preferred_element_type=jnp.float32
    )
    grad_v = jnp.einsum("ihpq,iphd->iqhd", probs_b, dctx_img, preferred_element_type=jnp.float32)
    flat = (rows_all, local_width)
    grad_q, grad_k, grad_v = (
        grad_q.astype(jnp.bfloat16).reshape(flat),
        grad_k.astype(jnp.bfloat16).reshape(flat),
        grad_v.astype(jnp.bfloat16).reshape(flat),
    )
    grad_weight = lax.psum_scatter(
        grad_total.astype(jnp.bfloat16).astype(jnp.float32).astype(jnp.bfloat16),
        "dp",
        scatter_dimension=1,
        tiled=True,
    ).astype(jnp.float32)
    new_master, new_one, new_two = adam_update(grad_weight, master, moment_one, moment_two)
    return (attn_out, grad_q, grad_k, grad_v, new_master, new_one, new_two)


def solution(mesh):
    in_specs = (
        P("dp", "mp"),
        P("dp", "mp"),
        P("dp", "mp"),
        P(("dp", "mp"), None),
        P("mp", "dp"),
        P("mp", "dp"),
        P("mp", "dp"),
    )
    out_specs = (
        P(("dp", "mp"), None),
        P("dp", "mp"),
        P("dp", "mp"),
        P("dp", "mp"),
        P("mp", "dp"),
        P("mp", "dp"),
        P("mp", "dp"),
    )
    return jax.shard_map(local, mesh=mesh, in_specs=in_specs, out_specs=out_specs, check_vma=False)
```

profile of v0, /device:TPU:19, one launch (start us, length us, event | category | flops | bytes accessed | tf_op | source)
XLA Modules:
  0.0 534.9 jit_solution(9344296823073232112)
XLA Ops:
  7.2 0.0 copy-start
  7.2 0.0 copy-start.2
  7.2 0.0 all-gather.5.cloned.1.call-start
  7.2 0.7 all-gather.5.cloned.1.call-update
  7.9 0.0 reduce-scatter.2.cloned.1.call-start
  8.0 1.2 copy.34
  9.2 0.0 copy-done.2
  9.2 0.2 copy.35
  9.4 2.1 fusion.47
  11.6 0.0 copy-done
  11.6 2.0 convolution_convert_fusion.2
  13.6 26.1 %all-gather.5.cloned.1.call-done = bf16[256,6144]{1,0:T(8,128)(2,1)} async-done(((bf16[64,6144]{1,0:T(8,128)(2,1)}), bf16[256,6144]{1,0:T(8,128)(2,1)}) %all-gather.5.cloned.1.call-update) | async-done | bytes 3145744 | tf_op jit(solution)/shard_map/all_gather | solution.py:58
  39.6 8.2 %convolution_convert_fusion = bf16[1024,6144]{1,0:T(8,128)(2,1)} fusion(bf16[256,1024]{0,1:T(8,128)(2,1)S(1)} %bitcast.55, bf16[256,6144]{1,0:T(8,128)(2,1)} %all-gather.5.cloned.1.call-done), kind=kOutput, calls=%fused_computation.6 | convolution fusion | flops 3227516928 | bytes 16252928 | tf_op jit(solution)/shard_map/tk,td->kd/dot_general | solution.py:60
  47.9 0.0 reduce-scatter.2.cloned.1.call-update
  47.9 0.2 all-gather.3.cloned.1.call-start
  48.1 206.0 %reduce-scatter.2.cloned.1.call-done = bf16[1024,768]{1,0:T(8,128)(2,1)} async-done(((bf16[1024,6144]{1,0:T(8,128)(2,1)}), bf16[1024,768]{1,0:T(8,128)(2,1)}) %reduce-scatter.2.cloned.1.call-update) | async-done | bytes 1572880 | tf_op jit(solution)/shard_map/reduce_scatter | solution.py:81
  254.1 9.6 %divide_subtract_fusion = (f32[1024,768]{1,0:T(8,128)}, f32[1024,768]{1,0:T(8,128)}, f32[1024,768]{1,0:T(8,128)}, bf16[1024,768]{1,0:T(8,128)(2,1)}) fusion(f32[1024,768]{1,0:T(8,128)} %param.13, bf16[1024,768]{1,0:T(8,128)(2,1)} %reduce-scatter.2.cloned.1.call-done, f32[1024,768]{1,0:T(8,128)} %param.14, f32[1024,768]{1,0:T(8,128)} %param.15), kind=kLoop, calls=%fused_computation.11 | loop fusion | flops 11010048 | bytes 22020096 | tf_op jit(solution)/shard_map/sub | solution.py:19
  263.7 0.0 all-gather.3.cloned.1.call-update
  263.7 0.2 copy.18
  263.9 173.8 %all-gather.3.cloned.1.call-done = bf16[1024,6144]{1,0:T(8,128)(2,1)} async-done(((bf16[1024,768]{1,0:T(8,128)(2,1)}), bf16[1024,6144]{1,0:T(8,128)(2,1)}) %all-gather.3.cloned.1.call-update) | async-done | bytes 12582928 | tf_op jit(solution)/shard_map/all_gather | solution.py:36
  437.8 9.8 %convolution_convert_fusion.1 = bf16[256,1024]{1,0:T(8,128)(2,1)} fusion(bf16[256,6144]{1,0:T(8,128)(2,1)} %all-gather.5.cloned.1.call-done, bf16[1024,6144]{1,0:T(8,128)(2,1)} %all-gather.3.cloned.1.call-done), kind=kOutput, calls=%fused_computation.22 | convolution fusion | flops 3221487616 | bytes 16252928 | tf_op jit(solution)/shard_map/td,kd->tk/dot_general | solution.py:61
  447.5 1.2 copy.36
  448.8 1.7 fusion.29
  450.5 5.0 fusion.22
  455.6 4.2 fusion.19
  459.8 0.0 copy-start.3
  459.8 2.9 convolution_convert_fusion.3
  462.7 0.0 copy-start.4
  462.7 0.0 copy-done.3
  462.7 1.0 copy.28
  463.7 1.0 copy.27
  464.7 0.0 copy-done.4
  464.7 1.0 copy.29
  465.8 7.0 %fusion.35 = bf16[64,6144]{1,0:T(8,128)(2,1)S(1)} fusion(bf16[1024,6144]{1,0:T(8,128)(2,1)} %all-gather.3.cloned.1.call-done, bf16[256,1024]{0,1:T(8,128)(2,1)S(1)} %bitcast.57, s32[]{:T(128)S(6)} %select_n.38), kind=kOutput, calls=%fused_computation.36 | convolution fusion | flops 805306368 | bytes 13631492 | tf_op jit(solution)/shard_map/dot_general | solution.py:48
  472.7 54.7 %while.15 = (s32[]{:T(128)}, bf16[64,6144]{1,0:T(8,128)(2,1)S(1)}, s32[]{:T(128)}, bf16[256,1024]{1,0:T(8,128)(2,1)S(1)}, bf16[1024,6144]{1,0:T(8,128)(2,1)}, /*...) while((s32[]{:T(128)}, bf16[64,6144]{1,0:T(8,128)(2,1)S(1)}, ...), condition=%wide.region_3.4_spmd, body=%wide.region_2.3_spmd.sunk | while | flops 806486016 | bytes 17432916 | solution.py:54
  472.8 2.2 collective-permute-start
  475.0 8.9 %collective-permute-done = bf16[64,6144]{1,0:T(8,128)(2,1)S(1)} collective-permute-done((bf16[64,6144]{1,0:T(8,128)(2,1)S(1)}, bf16[64,6144]{1,0:T(8,128)(2,1)S(1)}, u32[]{:S(2)}, u32[]{:S(2)}) %collective-permute-start) | collective-permute-done | bytes 786464 | tf_op jit(solution)/shard_map/while/body/eval_jaxpr/ppermute | solution.py:13
  483.9 6.9 %convert_add_fusion.2 = bf16[64,6144]{1,0:T(8,128)(2,1)S(1)} fusion(bf16[64,6144]{1,0:T(8,128)(2,1)S(1)} %collective-permute-done, bf16[1024,6144]{1,0:T(8,128)(2,1)} %get-tuple-element.229, bf16[256,1024]{1,0:T(8,128)(2,1)S(1)} %get-tuple-element.228, s32[]{:T(128)S(6)} %select_n.42), kind=kOutput, calls=%fused_computation.clone.1 | convolution fusion | flops 806486016 | bytes 14286852 | tf_op jit(solution)/shard_map/while/body/eval_jaxpr/dot_general | solution.py:48
  490.8 2.5 collective-permute-start
  493.3 8.9 %collective-permute-done = bf16[64,6144]{1,0:T(8,128)(2,1)S(1)} collective-permute-done((bf16[64,6144]{1,0:T(8,128)(2,1)S(1)}, bf16[64,6144]{1,0:T(8,128)(2,1)S(1)}, u32[]{:S(2)}, u32[]{:S(2)}) %collective-permute-start) | collective-permute-done | bytes 786464 | tf_op jit(solution)/shard_map/while/body/eval_jaxpr/ppermute | solution.py:13
  502.3 6.9 %convert_add_fusion.2 = bf16[64,6144]{1,0:T(8,128)(2,1)S(1)} fusion(bf16[64,6144]{1,0:T(8,128)(2,1)S(1)} %collective-permute-done, bf16[1024,6144]{1,0:T(8,128)(2,1)} %get-tuple-element.229, bf16[256,1024]{1,0:T(8,128)(2,1)S(1)} %get-tuple-element.228, s32[]{:T(128)S(6)} %select_n.42), kind=kOutput, calls=%fused_computation.clone.1 | convolution fusion | flops 806486016 | bytes 14286852 | tf_op jit(solution)/shard_map/while/body/eval_jaxpr/dot_general | solution.py:48
  509.1 2.5 collective-permute-start
  511.7 8.9 %collective-permute-done = bf16[64,6144]{1,0:T(8,128)(2,1)S(1)} collective-permute-done((bf16[64,6144]{1,0:T(8,128)(2,1)S(1)}, bf16[64,6144]{1,0:T(8,128)(2,1)S(1)}, u32[]{:S(2)}, u32[]{:S(2)}) %collective-permute-start) | collective-permute-done | bytes 786464 | tf_op jit(solution)/shard_map/while/body/eval_jaxpr/ppermute | solution.py:13
  520.6 6.9 %convert_add_fusion.2 = bf16[64,6144]{1,0:T(8,128)(2,1)S(1)} fusion(bf16[64,6144]{1,0:T(8,128)(2,1)S(1)} %collective-permute-done, bf16[1024,6144]{1,0:T(8,128)(2,1)} %get-tuple-element.229, bf16[256,1024]{1,0:T(8,128)(2,1)S(1)} %get-tuple-element.228, s32[]{:T(128)S(6)} %select_n.42), kind=kOutput, calls=%fused_computation.clone.1 | convolution fusion | flops 806486016 | bytes 14286852 | tf_op jit(solution)/shard_map/while/body/eval_jaxpr/dot_general | solution.py:48
  527.5 0.0 copy-start.1
  527.5 0.9 copy-done.1
Async XLA Ops:
  7.2 4.4 copy-start
  7.2 2.0 copy-start.2
  7.2 32.4 %all-gather.5.cloned.1.call-start = ((), (), s32[]{:S(2)}) async-start(), calls=%async_computation.2 | async-start | bytes 3932160 | tf_op jit(solution)/shard_map/all_gather | solution.py:58
  7.9 246.2 %reduce-scatter.2.cloned.1.call-start = ((), (), s32[]{:S(2)}) async-start(), calls=%async_computation.3 | async-start | bytes 14155776 | tf_op jit(solution)/shard_map/reduce_scatter | solution.py:81
  47.9 389.9 %all-gather.3.cloned.1.call-start = ((), (), s32[]{:S(2)}) async-start(), calls=%async_computation.1 | async-start | bytes 14155776 | tf_op jit(solution)/shard_map/all_gather | solution.py:36
  459.8 2.9 copy-start.3
  462.7 2.0 copy-start.4
  472.8 11.1 %collective-permute-start = (bf16[64,6144]{1,0:T(8,128)(2,1)S(1)}, bf16[64,6144]{1,0:T(8,128)(2,1)S(1)}, u32[]{:S(2)}, u32[]{:S(2)}) collective-permute-start(bf16[64,6144]{1,0:T(8,128)(2,1)S(1)} %get-tuple-element.214), channel_id=1, source_target_pairs={{3,0},{0,1},{1,2},{2,3},{7,4},{4,5},{5,6},{6,7},{11,8},{8,9},{9,10... | collective-permute-start | bytes 2359304 | tf_op jit(solution)/shard_map/while/body/eval_jaxpr/ppermute | solution.py:13
  490.8 11.5 %collective-permute-start = (bf16[64,6144]{1,0:T(8,128)(2,1)S(1)}, bf16[64,6144]{1,0:T(8,128)(2,1)S(1)}, u32[]{:S(2)}, u32[]{:S(2)}) collective-permute-start(bf16[64,6144]{1,0:T(8,128)(2,1)S(1)} %get-tuple-element.214), channel_id=1, source_target_pairs={{3,0},{0,1},{1,2},{2,3},{7,4},{4,5},{5,6},{6,7},{11,8},{8,9},{9,10... | collective-permute-start | bytes 2359304 | tf_op jit(solution)/shard_map/while/body/eval_jaxpr/ppermute | solution.py:13
  509.1 11.5 %collective-permute-start = (bf16[64,6144]{1,0:T(8,128)(2,1)S(1)}, bf16[64,6144]{1,0:T(8,128)(2,1)S(1)}, u32[]{:S(2)}, u32[]{:S(2)}) collective-permute-start(bf16[64,6144]{1,0:T(8,128)(2,1)S(1)} %get-tuple-element.214), channel_id=1, source_target_pairs={{3,0},{0,1},{1,2},{2,3},{7,4},{4,5},{5,6},{6,7},{11,8},{8,9},{9,10... | collective-permute-start | bytes 2359304 | tf_op jit(solution)/shard_map/while/body/eval_jaxpr/ppermute | solution.py:13
  527.5 0.9 copy-start.1
Sparse Core Ops, SparseCore 0:
  9.6 29.9 all-gather.4
  48.0 206.0 reduce-scatter.1
  263.8 173.8 all-gather.2
where the time goes:
time: 540 us; the launch traced here: 535 us
  waiting for transfers between devices  433 us (80%)
  matrix products  63.6 us (12%)
  between operations  13.9 us (3%)
  other arithmetic  9.56 us (2%)
  starting transfers between devices  7.58 us (1%)
  local copies, waits for them, and re-layouts  6.8 us (1%)
    reduce_scatter x1, waiting for transfers between devices, local(): lax.psum_scatter(grad_total.astype(jnp.bfloat16).astype(jnp.float32).asty...  206 us
    all_gather x1, waiting for transfers between devices, local(): lax.all_gather(master.astype(jnp.bfloat16), 'dp', axis=1, tiled=True)  174 us
    dot_general x4, matrix products, partial_rows(): return jnp.dot(ctx_rows, columns, preferred_element_type=jnp.float32)  27.6 us
    ppermute x3, waiting for transfers between devices, passed_along(): return lax.ppermute(block, axis, route)  26.8 us
    all_gather x1, waiting for transfers between devices, local(): piece = lax.all_gather(cotangent, 'mp', axis=0, tiled=True)  26.1 us
  transfers between devices with their start and end apart: 6, of which 6 were waited for; matrix products, arithmetic and copies ran while one was open for 1% of the time, Pallas kernels for 0%

commit v1 on v0

v1 whole, which is shorter than its diff:
```python
import functools

import jax
import jax.numpy as jnp
from jax import lax
from jax.experimental import pallas as pl
from jax.experimental.pallas import tpu as pltpu
from jax.sharding import PartitionSpec as P

HEAD_DIM = 128
PATCHES = 256
PAIR = 2
SCALING = HEAD_DIM ** (-0.5)
NT = (((1,), (1,)), ((), ()))
TN = (((0,), (0,)), ((), ()))


def dot(x, y, dims=(((1,), (0,)), ((), ()))):
    return lax.dot_general(x, y, dims, preferred_element_type=jnp.float32)


def softmax_of(q, k):
    scores = dot(q, k, NT) * SCALING
    e = jnp.exp(scores - jnp.max(scores, axis=-1, keepdims=True))
    return e / jnp.sum(e, axis=-1, keepdims=True)


def forward_kernel(q_ref, k_ref, v_ref, ctx_ref):
    probs = softmax_of(q_ref[...], k_ref[...]).astype(jnp.bfloat16)
    ctx_ref[...] = dot(probs, v_ref[...]).astype(jnp.bfloat16)


def backward_kernel(count, q_ref, k_ref, v_ref, *refs):
    parts, (gq_ref, gk_ref, gv_ref) = refs[:count], refs[count:]
    total = parts[0][...]
    for part in parts[1:]:
        total = total + part[...].astype(jnp.float32)
    dctx = total.astype(jnp.bfloat16)
    q, k = q_ref[...], k_ref[...]
    probs = softmax_of(q, k)
    grad_probs = dot(dctx, v_ref[...], NT)
    inner = jnp.sum(probs * grad_probs, axis=-1, keepdims=True)
    grad_scores = (probs * (grad_probs - inner) * SCALING).astype(jnp.bfloat16)
    gq_ref[...] = dot(grad_scores, k).astype(jnp.bfloat16)
    gk_ref[...] = dot(grad_scores, q, TN).astype(jnp.bfloat16)
    gv_ref[...] = dot(probs.astype(jnp.bfloat16), dctx, TN).astype(jnp.bfloat16)


def per_head(kernel, operands, outs):
    rows, width = operands[0].shape
    block = pl.BlockSpec((PATCHES, HEAD_DIM), lambda i, h: (i, h))
    shape = jax.ShapeDtypeStruct((rows, width), jnp.bfloat16)
    area = rows * PATCHES * width
    return pl.pallas_call(
        kernel,
        grid=(rows // PATCHES, width // HEAD_DIM),
        in_specs=[block] * len(operands),
        out_specs=[block] * outs,
        out_shape=[shape] * outs,
        cost_estimate=pl.CostEstimate(
            flops=4 * outs * area,
            bytes_accessed=2 * (len(operands) + outs) * rows * width,
            transcendentals=rows * PATCHES * width // HEAD_DIM,
        ),
    )(*operands)


def adam_update(grad_weight, master, moment_one, moment_two):
    new_one = 0.9 * moment_one + 0.1 * grad_weight
    new_two = 0.95 * moment_two + 0.05 * grad_weight * grad_weight
    new_master = master - 0.001 * (new_one / 0.19) / (jnp.sqrt(new_two / 0.0975) + 1e-08)
    return (new_master, new_one, new_two)


def local(queries, keys, values, cotangent, master, moment_one, moment_two):
    bf16 = jnp.bfloat16
    B = PAIR
    A = lax.axis_size("dp") // B
    M = lax.axis_size("mp")
    d = lax.axis_index("dp")
    a, b = d // B, d % B
    m = lax.axis_index("mp")
    rows, width = queries.shape
    S, D = cotangent.shape
    C = master.shape[1]
    W = B * C

    def along_a(x, t):
        route = [(i * B + j, ((i + t) % A) * B + j) for i in range(A) for j in range(B)]
        return lax.ppermute(x, "dp", route)

    def along_b(x):
        route = [(i * B + j, i * B + 1 - j) for i in range(A) for j in range(B)]
        return lax.ppermute(x, "dp", route)

    def along_m(x, t):
        return lax.ppermute(x, "mp", [(i, (i + t) % M) for i in range(M)])

    def pick(x, i):
        return lax.dynamic_index_in_dim(x, i, 0, keepdims=False)

    cot_blocks = cotangent.reshape(S, A, W).transpose(1, 0, 2)
    rows_of = jnp.zeros((A, S, W), bf16)
    rows_of = lax.dynamic_update_index_in_dim(rows_of, pick(cot_blocks, a), a, 0)
    for t in range(1, A):
        got = along_a(pick(cot_blocks, (a + t) % A), t)
        rows_of = lax.dynamic_update_index_in_dim(rows_of, got, (a - t) % A, 0)

    mine = master.astype(bf16)
    other = along_b(mine)
    weight = jnp.where(
        b == 0, jnp.concatenate([mine, other], 1), jnp.concatenate([other, mine], 1)
    )

    (context,) = per_head(forward_kernel, [queries, keys, values], 1)
    ctx_all = jnp.zeros((A, rows, width), bf16)
    ctx_all = lax.dynamic_update_index_in_dim(ctx_all, context, a, 0)
    for t in range(1, A):
        ctx_all = lax.dynamic_update_index_in_dim(ctx_all, along_a(context, t), (a - t) % A, 0)

    cot_all = jnp.zeros((A, M, S, W), bf16)
    cot_all = lax.dynamic_update_slice_in_dim(cot_all, rows_of[:, None], m, 1)
    for s in range(1, M):
        got = along_m(rows_of, s)
        cot_all = lax.dynamic_update_slice_in_dim(cot_all, got[:, None], (m - s) % M, 1)
    cot_all = cot_all.reshape(A, rows, W)

    part = jnp.einsum("atd,kd->atk", cot_all, weight, preferred_element_type=jnp.float32)
    terms = [pick(part, a)]
    part_b = part.astype(bf16)
    for t in range(1, A):
        terms.append(along_a(pick(part_b, (a + t) % A), t))

    ctx_flat = ctx_all.reshape(A, M, S, width)
    out = jnp.einsum("amsk,kd->masd", ctx_flat, weight, preferred_element_type=jnp.float32)
    total = pick(out, m)
    out_b = out.astype(bf16)
    for s in range(1, M):
        total = total + along_m(pick(out_b, (m + s) % M), s).astype(jnp.float32)
    summed = total.astype(bf16)
    attn = jnp.zeros((S, D), bf16)
    attn = lax.dynamic_update_slice_in_dim(attn, pick(summed, a), a * W, 1)
    for t in range(1, A):
        got = along_a(pick(summed, (a + t) % A), t)
        attn = lax.dynamic_update_slice_in_dim(attn, got, ((a - t) % A) * W, 1)

    grad = jnp.einsum("atk,atd->kd", ctx_all, cot_all, preferred_element_type=jnp.float32)
    keep = lax.dynamic_slice_in_dim(grad, b * C, C, 1)
    give = lax.dynamic_slice_in_dim(grad, (1 - b) * C, C, 1).astype(bf16)
    grad_weight = keep + along_b(give).astype(jnp.float32)
    news = adam_update(grad_weight, master, moment_one, moment_two)

    grads = per_head(
        functools.partial(backward_kernel, len(terms)), [queries, keys, values, *terms], 3
    )
    return (attn, *grads, *news)


def solution(mesh):
    in_specs = (
        P("dp", "mp"),
        P("dp", "mp"),
        P("dp", "mp"),
        P(("dp", "mp"), None),
        P("mp", "dp"),
        P("mp", "dp"),
        P("mp", "dp"),
    )
    out_specs = (
        P(("dp", "mp"), None),
        P("dp", "mp"),
        P("dp", "mp"),
        P("dp", "mp"),
        P("mp", "dp"),
        P("mp", "dp"),
        P("mp", "dp"),
    )
    return jax.shard_map(local, mesh=mesh, in_specs=in_specs, out_specs=out_specs, check_vma=False)
```

time: 540 us -> 294 us (0.54)
  waiting for transfers between devices: 433 us -> 201 us
  matrix products: 63.6 us -> 21.3 us
  Pallas kernels: 0 us -> 15.9 us
  local copies, waits for them, and re-layouts: 6.8 us -> 19.7 us
  between operations: 13.9 us -> 1.06 us
  starting transfers between devices: 7.58 us -> 19.1 us
    reduce_scatter x1 -> x0, waiting for transfers between devices: 206 us -> none  [local(): lax.psum_scatter(grad_total.astype(jnp.bfloat16).astype(jnp.float32).asty...]
    all_gather x2 -> x0, waiting for transfers between devices: 200 us -> none  [the longest x1 174 us: local(): lax.all_gather(master.astype(jnp.bfloat16), 'dp', axis=1, tiled=True)]
    ppermute x3 -> x20, waiting for transfers between devices: 26.8 us -> 201 us  [the longest x12 97.1 us: along_a(): return lax.ppermute(x, 'dp', route)]
    dot_general x11 -> x3, matrix products: 61.5 us -> 21.3 us  [the longest x1 9.18 us: local(): jnp.einsum('amsk,kd->masd', ctx_flat, weight, preferred_element_type=jnp....]
    pallas_call x0 -> x2, Pallas kernels: none -> 15.9 us  [per_head(): pl.pallas_call(kernel, grid=(rows // PATCHES, width // HEAD_DIM), in_spec...]
    ppermute x3 -> x20, starting transfers between devices: 7.28 us -> 19.1 us  [the longest x12 10.3 us: along_a(): return lax.ppermute(x, 'dp', route)]
  transfers between devices with their start and end apart: 6 -> 20, of which waited for: 6 -> 12; matrix products, arithmetic and copies ran while one was open for 1% -> 7% of each run, Pallas kernels for 0% -> 3%
where the time goes in v1:
time: 294 us; the launch traced here: 291 us
  waiting for transfers between devices  201 us (68%)
  matrix products  21.3 us (7%)
  local copies, waits for them, and re-layouts  19.7 us (7%)
  starting transfers between devices  19.1 us (6%)
  Pallas kernels  15.9 us (5%)
  other arithmetic  12.9 us (4%)
    ppermute x12, waiting for transfers between devices, along_a(): return lax.ppermute(x, 'dp', route)  97.1 us
    ppermute x2, waiting for transfers between devices, along_b(): return lax.ppermute(x, 'dp', route)  71.9 us
    ppermute x6, waiting for transfers between devices, along_m(): return lax.ppermute(x, 'mp', [(i, (i + t) % M) for i in range(M)])  32.4 us
    pallas_call x2, Pallas kernels, per_head(): pl.pallas_call(kernel, grid=(rows // PATCHES, width // HEAD_DIM), in_spec...  15.9 us
    sub x1, other arithmetic, adam_update(): master - 0.001 * (new_one / 0.19) / (jnp.sqrt(new_two / 0.0975) + 1e-08)  11.1 us
    ppermute x12, starting transfers between devices, along_a(): return lax.ppermute(x, 'dp', route)  10.3 us
    dot_general x1, matrix products, local(): jnp.einsum('amsk,kd->masd', ctx_flat, weight, preferred_element_type=jnp....  9.18 us
    dot_general x1, matrix products, local(): jnp.einsum('atd,kd->atk', cot_all, weight, preferred_element_type=jnp.flo...  8.59 us
  transfers between devices with their start and end apart: 20, of which 12 were waited for; matrix products, arithmetic and copies ran while one was open for 7% of the time, Pallas kernels for 3%

profile of v1, /device:TPU:19, one launch (start us, length us, event | category | flops | bytes accessed | tf_op | source)
XLA Modules:
  0.0 291.4 jit_solution(14936416885705251117)
XLA Ops:
  0.6 7.2 %shard_map.126 = bf16[256,1024]{1,0:T(8,128)(2,1)} custom-call(bf16[256,1024]{1,0:T(8,128)(2,1)} %q_ref.3, bf16[256,1024]{1,0:T(8,128)(2,1)} %k_ref.3, bf16[256,1024]{1,0:T(8,128)(2,1)} %v_ref.3), custom_call_target="tpu_custom_call" | custom-call | flops 268435456 | bytes 2097152 | tf_op jit(solution)/shard_map/pallas_call | solution.py:54
  7.8 1.3 collective-permute-start.1
  9.1 0.1 collective-permute-start.2
  9.2 1.1 collective-permute-start.3
  10.3 2.3 reshape.31
  12.6 1.6 constant_dynamic-slice_fusion
  14.3 0.0 copy-start.5
  14.3 0.7 copy.48
  15.0 0.3 collective-permute-start.10
  15.3 0.7 copy.47
  16.0 2.3 collective-permute-start.11
  18.3 0.7 copy.46
  19.0 0.1 broadcast_in_dim.55
  19.2 0.3 broadcast_in_dim.49
  19.5 47.7 %collective-permute-done.10 = bf16[64,1536]{1,0:T(8,128)(2,1)S(1)} collective-permute-done((bf16[64,1536]{1,0:T(8,128)(2,1)}, bf16[64,1536]{1,0:T(8,128)(2,1)S(1)}, u32[]{:S(2)}, u32[]{:S(2)}) %collective-permute-start.10) | collective-permute-done | bytes 196640 | tf_op jit(solution)/shard_map/ppermute | solution.py:90
  67.2 4.5 %collective-permute-done.12 = bf16[64,1536]{1,0:T(8,128)(2,1)S(1)} collective-permute-done((bf16[64,1536]{1,0:T(8,128)(2,1)S(1)}, bf16[64,1536]{1,0:T(8,128)(2,1)S(1)}, u32[]{:S(2)}, u32[]{:S(2)}) %collective-permute-start.12) | collective-permute-done | bytes 196640 | tf_op jit(solution)/shard_map/ppermute | solution.py:90
  71.7 5.0 %collective-permute-start.13 = (bf16[4,64,1536]{2,1,0:T(8,128)(2,1)S(1)}, bf16[4,64,1536]{2,1,0:T(8,128)(2,1)S(1)}, u32[]{:S(2)}, u32[]{:S(2)}) collective-permute-start(bf16[4,64,1536]{2,1,0:T(8,128)(2,1)S(1)} %bitcast_dynamic-update-slice_fusion.9), channel_id=1, source_target_pairs={{0,1},{1,2},{2,3},{3,0},{4,5},{5,6},{6,7},{7,4},{8,9},{9,10},{10,1... | collective-permute-start | bytes 2359304 | tf_op jit(solution)/shard_map/ppermute | solution.py:97
  76.7 0.2 collective-permute-start.14
  77.0 0.3 broadcast_in_dim.54
  77.3 0.1 bitcast_dynamic-update-slice_fusion.3
  77.3 0.0 collective-permute-done.1
  77.3 0.5 collective-permute-start.15
  77.8 1.1 bitcast_dynamic-update-slice_fusion.6
  79.0 0.0 collective-permute-done.3
  79.0 14.4 %collective-permute-done.13 = bf16[4,64,1536]{2,1,0:T(8,128)(2,1)S(1)} collective-permute-done((bf16[4,64,1536]{2,1,0:T(8,128)(2,1)S(1)}, bf16[4,64,1536]{2,1,0:T(8,128)(2,1)S(1)}, u32[]{:S(2)}, u32[]{:S(2)}) %collective-permute-start.13) | collective-permute-done | bytes 786464 | tf_op jit(solution)/shard_map/ppermute | solution.py:97
  93.5 0.1 bitcast_dynamic-update-slice_fusion.2
  93.6 17.5 %collective-permute-done.14 = bf16[4,64,1536]{2,1,0:T(8,128)(2,1)S(1)} collective-permute-done((bf16[4,64,1536]{2,1,0:T(8,128)(2,1)S(1)}, bf16[4,64,1536]{2,1,0:T(8,128)(2,1)S(1)}, u32[]{:S(2)}, u32[]{:S(2)}) %collective-permute-start.14) | collective-permute-done | bytes 786464 | tf_op jit(solution)/shard_map/ppermute | solution.py:97
  111.0 0.1 bitcast_dynamic-update-slice_fusion.1
  111.1 0.5 collective-permute-done.15
  111.6 0.1 bitcast_dynamic-update-slice_fusion
  111.7 3.5 %convolution_bitcast_fusion = f32[1024,1536]{1,0:T(8,128)S(1)} fusion(bf16[4,256,1024]{2,1,0:T(8,128)(2,1)S(1)} %bitcast_dynamic-update-slice_fusion.4, bf16[4,256,1536]{2,1,0:T(8,128)(2,1)S(1)} %bitcast.97), kind=kOutput, calls=%fused_computation.1 | convolution fusion | flops 3221225472 | bytes 11534336 | tf_op jit(solution)/shard_map/atk,atd->kd/dot_general | solution.py:147
  115.2 2.6 copy-done
  117.9 1.3 dynamic-slice_convert_fusion
  119.2 0.3 collective-permute-start.19
  119.5 36.3 %collective-permute-done.19 = bf16[1024,768]{1,0:T(8,128)(2,1)} collective-permute-done((bf16[1024,768]{1,0:T(8,128)(2,1)}, bf16[1024,768]{1,0:T(8,128)(2,1)}, u32[]{:S(2)}, u32[]{:S(2)}) %collective-permute-start.19) | collective-permute-done | bytes 1572896 | tf_op jit(solution)/shard_map/ppermute | solution.py:94
  155.7 11.1 %divide_subtract_fusion = (f32[1024,768]{1,0:T(8,128)}, f32[1024,768]{1,0:T(8,128)}, f32[1024,768]{1,0:T(8,128)}, bf16[1024,768]{1,0:T(8,128)(2,1)}) fusion(f32[1024,768]{1,0:T(8,128)} %param.11, bf16[1024,768]{1,0:T(8,128)(2,1)} %collective-permute-done.19, f32[1024,1536]{1,0:T(8,128)} %copy-done, s32[]{:T(128)S(6)} %select_n.206, f32[1024,768]{1,0:T(8,128)} %param.12, ...), kind=kLoop, calls=%fused_computation.8 | loop fusion | flops 11796480 | bytes 25165828 | tf_op jit(solution)/shard_map/sub | solution.py:71
  166.8 0.1 collective-permute-start
  166.9 35.6 %collective-permute-done = bf16[1024,768]{1,0:T(8,128)(2,1)} collective-permute-done((bf16[1024,768]{1,0:T(8,128)(2,1)}, bf16[1024,768]{1,0:T(8,128)(2,1)}, u32[]{:S(2)}, u32[]{:S(2)}) %collective-permute-start) | collective-permute-done | bytes 1572896 | tf_op jit(solution)/shard_map/ppermute | solution.py:94
  202.6 8.6 %fusion.12 = (bf16[4,256,1024]{2,1,0:T(8,128)(2,1)S(1)}, f32[4,256,1024]{2,1,0:T(8,128)}) fusion(bf16[4,256,1536]{2,1,0:T(8,128)(2,1)S(1)} %bitcast.98, bf16[1024,768]{1,0:T(8,128)(2,1)} %get-tuple-element.16, bf16[1024,768]{1,0:T(8,128)(2,1)} %collective-permute-done, pred[]{:T(512)S(6)} %eq.29), kind=kOutput, calls=%fused_computation.52 | convolution fusion | flops 3236429824 | bytes 12582913 | tf_op jit(solution)/shard_map/atd,kd->atk/dot_general | solution.py:128
  211.2 1.1 dynamic-slice_bitcast_fusion.4
  212.2 0.0 collective-permute-start.16
  212.2 0.9 copy-done.4
  213.1 9.2 %fusion.11 = (bf16[1536,4,4,64]{0,3,2,1:T(8,128)(2,1)S(1)}, f32[1536,4,4,64]{0,3,2,1:T(8,128)}) fusion(bf16[4,4,64,1024]{3,2,1,0:T(8,128)(2,1)S(1)} %bitcast.99, bf16[1024,768]{1,0:T(8,128)(2,1)} %get-tuple-element.16, bf16[1024,768]{1,0:T(8,128)(2,1)} %collective-permute-done, pred[]{:T(512)S(6)} %eq.29), kind=kOutput, calls=%fused_computation.51 | convolution fusion | flops 3236954112 | bytes 14680065 | tf_op jit(solution)/shard_map/amsk,kd->masd/dot_general | solution.py:135
  222.3 1.3 dynamic-slice_bitcast_fusion.3
  223.6 1.6 collective-permute-start.4
  225.3 1.1 collective-permute-start.5
  226.4 0.3 collective-permute-start.17
  226.7 0.0 collective-permute-done.16.refs_1_
  226.7 0.8 copy-done.7
  227.6 0.8 collective-permute-start.18
  228.4 2.3 dynamic-slice_bitcast_fusion.refs_0_
  230.7 18.2 %collective-permute-done.17.refs_2_ = bf16[256,1024]{1,0:T(8,128)(2,1)} collective-permute-done((bf16[256,1024]{1,0:T(8,128)(2,1)}, bf16[256,1024]{1,0:T(8,128)(2,1)}, u32[]{:S(2)}, u32[]{:S(2)}) %collective-permute-start.17) | collective-permute-done | bytes 524320 | tf_op jit(solution)/shard_map/ppermute | solution.py:90
  248.9 11.2 %collective-permute-done.18.refs_3_ = bf16[256,1024]{1,0:T(8,128)(2,1)} collective-permute-done((bf16[256,1024]{1,0:T(8,128)(2,1)}, bf16[256,1024]{1,0:T(8,128)(2,1)}, u32[]{:S(2)}, u32[]{:S(2)}) %collective-permute-start.18) | collective-permute-done | bytes 524320 | tf_op jit(solution)/shard_map/ppermute | solution.py:90
  260.1 8.7 %shard_map.127 = (bf16[256,1024]{1,0:T(8,128)(2,1)}, bf16[256,1024]{1,0:T(8,128)(2,1)}, bf16[256,1024]{1,0:T(8,128)(2,1)}) custom-call(bf16[256,1024]{1,0:T(8,128)(2,1)} %q_ref.3, bf16[256,1024]{1,0:T(8,128)(2,1)} %k_ref.3, bf16[256,1024]{1,0:T(8,128)(2,1)} %v_ref.3, f32[256,1024]{1,0:T(8,128)} %dynamic-slice_bitcast_fusion.refs_0_, ...), custom_call_target="tpu_custom_call" | custom-call | flops 805306368 | bytes 5242880 | tf_op jit(solution)/shard_map/pallas_call | solution.py:54
  268.9 1.8 fusion.7
  270.7 2.8 collective-permute-start.7
  273.5 0.7 collective-permute-start.8
  274.2 0.6 collective-permute-start.9
  274.8 0.1 broadcast_in_dim.48
  274.9 1.8 collective-permute-done.7
  276.6 9.6 %collective-permute-done.8 = bf16[64,1536]{1,0:T(8,128)(2,1)S(1)} collective-permute-done((bf16[64,1536]{1,0:T(8,128)(2,1)S(1)}, bf16[64,1536]{1,0:T(8,128)(2,1)S(1)}, u32[]{:S(2)}, u32[]{:S(2)}) %collective-permute-start.8) | collective-permute-done | bytes 196640 | tf_op jit(solution)/shard_map/ppermute | solution.py:90
  286.3 4.2 %collective-permute-done.9 = bf16[64,1536]{1,0:T(8,128)(2,1)S(1)} collective-permute-done((bf16[64,1536]{1,0:T(8,128)(2,1)S(1)}, bf16[64,1536]{1,0:T(8,128)(2,1)S(1)}, u32[]{:S(2)}, u32[]{:S(2)}) %collective-permute-start.9) | collective-permute-done | bytes 196640 | tf_op jit(solution)/shard_map/ppermute | solution.py:90
  290.5 0.0 copy-start.6
  290.5 0.9 copy-done.6
  (31 shorter events, 0.4 us)
Async XLA Ops:
  7.8 69.5 %collective-permute-start.1 = (bf16[256,1024]{1,0:T(8,128)(2,1)}, bf16[256,1024]{1,0:T(8,128)(2,1)}, u32[]{:S(2)}, u32[]{:S(2)}) collective-permute-start(bf16[256,1024]{1,0:T(8,128)(2,1)} %shard_map.126), channel_id=1, source_target_pairs={{0,8},{4,12},{8,16},{12,20},{16,24},{20,28},{24,0},{28,4},{1,9},{5... | collective-permute-start | bytes 1572872 | tf_op jit(solution)/shard_map/ppermute | solution.py:90
  9.1 69.8 %collective-permute-start.2 = (bf16[256,1024]{1,0:T(8,128)(2,1)}, bf16[256,1024]{1,0:T(8,128)(2,1)S(1)}, u32[]{:S(2)}, u32[]{:S(2)}) collective-permute-start(bf16[256,1024]{1,0:T(8,128)(2,1)} %shard_map.126), channel_id=1, source_target_pairs={{0,16},{4,20},{8,24},{12,28},{16,0},{20,4},{24,8},{28,12},{1,17},{... | collective-permute-start | bytes 1572872 | tf_op jit(solution)/shard_map/ppermute | solution.py:90
  9.2 69.8 %collective-permute-start.3 = (bf16[256,1024]{1,0:T(8,128)(2,1)}, bf16[256,1024]{1,0:T(8,128)(2,1)S(1)}, u32[]{:S(2)}, u32[]{:S(2)}) collective-permute-start(bf16[256,1024]{1,0:T(8,128)(2,1)} %shard_map.126), channel_id=1, source_target_pairs={{0,24},{4,28},{8,0},{12,4},{16,8},{20,12},{24,16},{28,20},{1,25},{... | collective-permute-start | bytes 1572872 | tf_op jit(solution)/shard_map/ppermute | solution.py:90
  14.3 5.2 %copy-start.5 = (bf16[256,1024]{1,0:T(8,128)(2,1)S(1)}, bf16[256,1024]{1,0:T(8,128)(2,1)}, u32[]{:S(2)}) copy-start(bf16[256,1024]{1,0:T(8,128)(2,1)} %shard_map.126) | copy-start | bytes 1572868
  15.0 52.2 %collective-permute-start.10 = (bf16[64,1536]{1,0:T(8,128)(2,1)}, bf16[64,1536]{1,0:T(8,128)(2,1)S(1)}, u32[]{:S(2)}, u32[]{:S(2)}) collective-permute-start(bf16[64,1536]{1,0:T(8,128)(2,1)} %bitcast.96), channel_id=1, source_target_pairs={{0,8},{4,12},{8,16},{12,20},{16,24},{20,28},{24,0},{28,4},{1,9},{5... | collective-permute-start | bytes 589832 | tf_op jit(solution)/shard_map/ppermute | solution.py:90
  16.0 51.2 %collective-permute-start.11 = (bf16[64,1536]{1,0:T(8,128)(2,1)}, bf16[64,1536]{1,0:T(8,128)(2,1)S(1)}, u32[]{:S(2)}, u32[]{:S(2)}) collective-permute-start(bf16[64,1536]{1,0:T(8,128)(2,1)} %bitcast.95), channel_id=1, source_target_pairs={{0,16},{4,20},{8,24},{12,28},{16,0},{20,4},{24,8},{28,12},{1,17},{... | collective-permute-start | bytes 589832 | tf_op jit(solution)/shard_map/ppermute | solution.py:90
  19.0 48.1 %copy-start.8 = (bf16[64,1,1536]{2,0,1:T(8,128)(2,1)S(1)}, bf16[64,1,1536]{2,0,1:T(8,128)(2,1)}, u32[]{:S(2)}) copy-start(bf16[64,1,1536]{2,0,1:T(8,128)(2,1)} %copy.46) | copy-start | bytes 589828
  67.2 4.5 %collective-permute-start.12 = (bf16[64,1536]{1,0:T(8,128)(2,1)S(1)}, bf16[64,1536]{1,0:T(8,128)(2,1)S(1)}, u32[]{:S(2)}, u32[]{:S(2)}) collective-permute-start(bf16[64,1536]{1,0:T(8,128)(2,1)S(1)} %bitcast.100), channel_id=1, source_target_pairs={{0,24},{4,28},{8,0},{12,4},{16,8},{20,12},{24,16},{28,20},{1,25},{... | collective-permute-start | bytes 589832 | tf_op jit(solution)/shard_map/ppermute | solution.py:90
  71.7 21.8 %collective-permute-start.13 = (bf16[4,64,1536]{2,1,0:T(8,128)(2,1)S(1)}, bf16[4,64,1536]{2,1,0:T(8,128)(2,1)S(1)}, u32[]{:S(2)}, u32[]{:S(2)}) collective-permute-start(bf16[4,64,1536]{2,1,0:T(8,128)(2,1)S(1)} %bitcast_dynamic-update-slice_fusion.9), channel_id=1, source_target_pairs={{0,1},{1,2},{2,3},{3,0},{4,5},{5,6},{6,7},{7,4},{8,9},{9,10},{10,1... | collective-permute-start | bytes 2359304 | tf_op jit(solution)/shard_map/ppermute | solution.py:97
  76.7 34.3 %collective-permute-start.14 = (bf16[4,64,1536]{2,1,0:T(8,128)(2,1)S(1)}, bf16[4,64,1536]{2,1,0:T(8,128)(2,1)S(1)}, u32[]{:S(2)}, u32[]{:S(2)}) collective-permute-start(bf16[4,64,1536]{2,1,0:T(8,128)(2,1)S(1)} %bitcast_dynamic-update-slice_fusion.9), channel_id=1, source_target_pairs={{0,2},{1,3},{2,0},{3,1},{4,6},{5,7},{6,4},{7,5},{8,10},{9,11},{10,... | collective-permute-start | bytes 2359304 | tf_op jit(solution)/shard_map/ppermute | solution.py:97
  77.3 34.3 %collective-permute-start.15 = (bf16[4,64,1536]{2,1,0:T(8,128)(2,1)S(1)}, bf16[4,64,1536]{2,1,0:T(8,128)(2,1)S(1)}, u32[]{:S(2)}, u32[]{:S(2)}) collective-permute-start(bf16[4,64,1536]{2,1,0:T(8,128)(2,1)S(1)} %bitcast_dynamic-update-slice_fusion.9), channel_id=1, source_target_pairs={{0,3},{1,0},{2,1},{3,2},{4,7},{5,4},{6,5},{7,6},{8,11},{9,8},{10,9... | collective-permute-start | bytes 2359304 | tf_op jit(solution)/shard_map/ppermute | solution.py:97
  79.0 36.2 %copy-start.3 = (bf16[4,256,1024]{2,1,0:T(8,128)(2,1)}, bf16[4,256,1024]{2,1,0:T(8,128)(2,1)S(1)}, u32[]{:S(2)}) copy-start(bf16[4,256,1024]{2,1,0:T(8,128)(2,1)S(1)} %bitcast_dynamic-update-slice_fusion.4) | copy-start | bytes 6291460
  111.7 3.5 %copy-start.1 = (bf16[4,4,64,1536]{3,2,1,0:T(8,128)(2,1)}, bf16[4,4,64,1536]{3,2,1,0:T(8,128)(2,1)S(1)}, u32[]{:S(2)}) copy-start(bf16[4,4,64,1536]{3,2,1,0:T(8,128)(2,1)S(1)} %bitcast_dynamic-update-slice_fusion) | copy-start | bytes 9437188
  115.2 2.6 copy-start
  119.2 36.5 %collective-permute-start.19 = (bf16[1024,768]{1,0:T(8,128)(2,1)}, bf16[1024,768]{1,0:T(8,128)(2,1)}, u32[]{:S(2)}, u32[]{:S(2)}) collective-permute-start(bf16[1024,768]{1,0:T(8,128)(2,1)} %dynamic-slice_convert_fusion), channel_id=1, source_target_pairs={{0,4},{4,0},{8,12},{12,8},{16,20},{20,16},{24,28},{28,24},{1,5},{5... | collective-permute-start | bytes 4718600 | tf_op jit(solution)/shard_map/ppermute | solution.py:94
  119.5 83.1 %copy-start.2 = (bf16[4,4,64,1536]{3,2,1,0:T(8,128)(2,1)S(1)}, bf16[4,4,64,1536]{3,2,1,0:T(8,128)(2,1)}, u32[]{:S(2)}) copy-start(bf16[4,4,64,1536]{3,2,1,0:T(8,128)(2,1)} %copy-done.1) | copy-start | bytes 9437188
  166.8 35.7 %collective-permute-start = (bf16[1024,768]{1,0:T(8,128)(2,1)}, bf16[1024,768]{1,0:T(8,128)(2,1)}, u32[]{:S(2)}, u32[]{:S(2)}) collective-permute-start(bf16[1024,768]{1,0:T(8,128)(2,1)} %get-tuple-element.16), channel_id=1, source_target_pairs={{0,4},{4,0},{8,12},{12,8},{16,20},{20,16},{24,28},{28,24},{1,5},{5... | collective-permute-start | bytes 4718600 | tf_op jit(solution)/shard_map/ppermute | solution.py:94
  211.1 2.0 copy-start.4
  212.2 14.5 %collective-permute-start.16 = (bf16[256,1024]{1,0:T(8,128)(2,1)S(1)}, bf16[256,1024]{1,0:T(8,128)(2,1)S(1)}, u32[]{:S(2)}, u32[]{:S(2)}) collective-permute-start(bf16[256,1024]{1,0:T(8,128)(2,1)S(1)} %get-tuple-element.22), channel_id=1, source_target_pairs={{0,8},{4,12},{8,16},{12,20},{16,24},{20,28},{24,0},{28,4},{1,9},{5... | collective-permute-start | bytes 1572872 | tf_op jit(solution)/shard_map/ppermute | solution.py:90
  223.6 45.2 %collective-permute-start.4 = (bf16[4,64,1536]{2,1,0:T(8,128)(2,1)}, bf16[4,64,1536]{2,1,0:T(8,128)(2,1)S(1)}, u32[]{:S(2)}, u32[]{:S(2)}) collective-permute-start(bf16[4,64,1536]{2,1,0:T(8,128)(2,1)} %get-tuple-element.17), channel_id=1, source_target_pairs={{0,1},{1,2},{2,3},{3,0},{4,5},{5,6},{6,7},{7,4},{8,9},{9,10},{10,1... | collective-permute-start | bytes 2359304 | tf_op jit(solution)/shard_map/ppermute | solution.py:97
  225.3 43.6 %collective-permute-start.5 = (bf16[4,64,1536]{2,1,0:T(8,128)(2,1)}, bf16[4,64,1536]{2,1,0:T(8,128)(2,1)S(1)}, u32[]{:S(2)}, u32[]{:S(2)}) collective-permute-start(bf16[4,64,1536]{2,1,0:T(8,128)(2,1)} %get-tuple-element.19), channel_id=1, source_target_pairs={{0,2},{1,3},{2,0},{3,1},{4,6},{5,7},{6,4},{7,5},{8,10},{9,11},{10,... | collective-permute-start | bytes 2359304 | tf_op jit(solution)/shard_map/ppermute | solution.py:97
  226.4 42.5 %collective-permute-start.6 = (bf16[4,64,1536]{2,1,0:T(8,128)(2,1)S(1)}, bf16[4,64,1536]{2,1,0:T(8,128)(2,1)S(1)}, u32[]{:S(2)}, u32[]{:S(2)}) collective-permute-start(bf16[4,64,1536]{2,1,0:T(8,128)(2,1)S(1)} %get-tuple-element.18), channel_id=1, source_target_pairs={{0,3},{1,0},{2,1},{3,2},{4,7},{5,4},{6,5},{7,6},{8,11},{9,8},{10,9... | collective-permute-start | bytes 2359304 | tf_op jit(solution)/shard_map/ppermute | solution.py:97
  226.4 22.5 %collective-permute-start.17 = (bf16[256,1024]{1,0:T(8,128)(2,1)}, bf16[256,1024]{1,0:T(8,128)(2,1)}, u32[]{:S(2)}, u32[]{:S(2)}) collective-permute-start(bf16[256,1024]{1,0:T(8,128)(2,1)} %get-tuple-element.21), channel_id=1, source_target_pairs={{0,16},{4,20},{8,24},{12,28},{16,0},{20,4},{24,8},{28,12},{1,17},{... | collective-permute-start | bytes 1572872 | tf_op jit(solution)/shard_map/ppermute | solution.py:90
  226.7 0.8 copy-start.7
  227.6 32.5 %collective-permute-start.18 = (bf16[256,1024]{1,0:T(8,128)(2,1)}, bf16[256,1024]{1,0:T(8,128)(2,1)}, u32[]{:S(2)}, u32[]{:S(2)}) collective-permute-start(bf16[256,1024]{1,0:T(8,128)(2,1)} %get-tuple-element.20), channel_id=1, source_target_pairs={{0,24},{4,28},{8,0},{12,4},{16,8},{20,12},{24,16},{28,20},{1,25},{... | collective-permute-start | bytes 1572872 | tf_op jit(solution)/shard_map/ppermute | solution.py:90
  270.7 5.9 %collective-permute-start.7 = (bf16[64,1536]{1,0:T(8,128)(2,1)S(1)}, bf16[64,1536]{1,0:T(8,128)(2,1)S(1)}, u32[]{:S(2)}, u32[]{:S(2)}) collective-permute-start(bf16[64,1536]{1,0:T(8,128)(2,1)S(1)} %get-tuple-element.29), channel_id=1, source_target_pairs={{0,8},{4,12},{8,16},{12,20},{16,24},{20,28},{24,0},{28,4},{1,9},{5... | collective-permute-start | bytes 589832 | tf_op jit(solution)/shard_map/ppermute | solution.py:90
  273.5 12.8 %collective-permute-start.8 = (bf16[64,1536]{1,0:T(8,128)(2,1)S(1)}, bf16[64,1536]{1,0:T(8,128)(2,1)S(1)}, u32[]{:S(2)}, u32[]{:S(2)}) collective-permute-start(bf16[64,1536]{1,0:T(8,128)(2,1)S(1)} %get-tuple-element.28), channel_id=1, source_target_pairs={{0,16},{4,20},{8,24},{12,28},{16,0},{20,4},{24,8},{28,12},{1,17},{... | collective-permute-start | bytes 589832 | tf_op jit(solution)/shard_map/ppermute | solution.py:90
  274.2 16.3 %collective-permute-start.9 = (bf16[64,1536]{1,0:T(8,128)(2,1)S(1)}, bf16[64,1536]{1,0:T(8,128)(2,1)S(1)}, u32[]{:S(2)}, u32[]{:S(2)}) collective-permute-start(bf16[64,1536]{1,0:T(8,128)(2,1)S(1)} %get-tuple-element.27), channel_id=1, source_target_pairs={{0,24},{4,28},{8,0},{12,4},{16,8},{20,12},{24,16},{28,20},{1,25},{... | collective-permute-start | bytes 589832 | tf_op jit(solution)/shard_map/ppermute | solution.py:90
  290.5 0.9 copy-start.6

commit v2 on v0

v2 whole, which is shorter than its diff:
```python
import functools

import jax
import jax.numpy as jnp
from jax import lax
from jax.experimental import pallas as pl
from jax.experimental.pallas import tpu as pltpu
from jax.sharding import PartitionSpec as P

HEAD_DIM = 128
PATCHES = 256
PAIR = 2
SCALING = HEAD_DIM ** (-0.5)
NT = (((1,), (1,)), ((), ()))
TN = (((0,), (0,)), ((), ()))


def dot(x, y, dims=(((1,), (0,)), ((), ()))):
    return lax.dot_general(x, y, dims, preferred_element_type=jnp.float32)


def softmax_of(q, k):
    scores = dot(q, k, NT) * SCALING
    e = jnp.exp(scores - jnp.max(scores, axis=-1, keepdims=True))
    return e / jnp.sum(e, axis=-1, keepdims=True)


MESH = pl.DeviceIdType.MESH


def tiles_of(extent, size=256):
    return size if extent % size == 0 else extent


def main_kernel(
    A, M, q_ref, k_ref, v_ref, cotb, wb,
    attn_ref, gq_ref, gk_ref, gv_ref, gw_ref,
    w2, cot_all, ctx_all, gbuf, grecv, gown, obuf, orecv, oown, summed, arecv, gwbuf, gwrecv,
    w_s, w_r, cz_s, cz_r, cy_s, cy_r, x_s, x_r, g_s, g_r, o_s, o_r, z_s, z_r, h_s, h_r,
):
    bf16, f32 = jnp.bfloat16, jnp.float32
    B = PAIR
    d, m = lax.axis_index("dp"), lax.axis_index("mp")
    a, b = d // B, d % B
    rows, width = q_ref.shape
    S, C = cotb.shape[2:]
    heads = width // HEAD_DIM

    def at_a(i):
        return (i * B + b, m)

    def at_m(i):
        return (d, i)

    partner = (a * B + 1 - b, m)

    def up_a(t):
        return lax.rem(a + t, A)

    def down_a(t):
        return lax.rem(a + A - t, A)

    def up_m(s):
        return lax.rem(m + s, M)

    def down_m(s):
        return lax.rem(m + M - s, M)

    def copy(src, dst, send, recv, device):
        return pltpu.make_async_remote_copy(
            src_ref=src, dst_ref=dst, send_sem=send, recv_sem=recv,
            device_id=device, device_id_type=MESH,
        )

    barrier = pltpu.get_barrier_semaphore()
    peers = [at_a(up_a(t)) for t in range(1, A)] + [at_m(up_m(s)) for s in range(1, M)] + [partner]
    for peer in peers:
        pl.semaphore_signal(barrier, inc=1, device_id=peer, device_id_type=MESH)
    pl.semaphore_wait(barrier, len(peers))

    sent = []

    def send(*args):
        c = copy(*args)
        c.start()
        sent.append(c)

    def arrived(slot, recv, device):
        copy(slot, slot, recv, recv, device).wait_recv()

    for t in range(1, A):
        to = up_a(t)
        send(cotb.at[to], cot_all.at[:, a, m], cz_s.at[t], cz_r.at[t], at_a(to))
    send(wb, w2.at[b], w_s.at[0], w_r.at[0], partner)
    for j in range(B):
        cot_all[j, a, m] = cotb[a, j]
    w2[b] = wb[...]

    def spread(t):
        here = down_a(t)
        for s in range(1, M):
            slot = cot_all.at[:, here, m]
            send(slot, slot, cy_s.at[t, s], cy_r.at[t, s], at_m(up_m(s)))

    spread(0)

    @pl.loop(0, heads)
    def _(h):
        cols = pl.ds(pl.multiple_of(h * HEAD_DIM, HEAD_DIM), HEAD_DIM)
        for i in range(rows // PATCHES):
            r = pl.ds(i * PATCHES, PATCHES)
            probs = softmax_of(q_ref[r, cols], k_ref[r, cols]).astype(bf16)
            ctx_all[a, r, cols] = dot(probs, v_ref[r, cols]).astype(bf16)

    for t in range(1, A):
        arrived(cot_all.at[:, down_a(t), m], cz_r.at[t], at_a(down_a(t)))
        spread(t)
    for t in range(1, A):
        send(ctx_all.at[a], ctx_all.at[a], x_s.at[t], x_r.at[t], at_a(up_a(t)))

    arrived(w2.at[1 - b], w_r.at[0], partner)
    kt = tiles_of(width)
    for t in [*range(1, A), 0]:
        for_a = up_a(t)
        from_t = (A - t) % A
        for s in range(1, M):
            arrived(cot_all.at[:, for_a, down_m(s)], cy_r.at[from_t, s], at_m(down_m(s)))

        @pl.loop(0, width // kt)
        def _(i):
            ks = pl.ds(pl.multiple_of(i * kt, kt), kt)
            total = dot(cot_all[0, for_a].reshape(rows, C), w2[0, ks, :], NT)
            for j in range(1, B):
                total = total + dot(cot_all[j, for_a].reshape(rows, C), w2[j, ks, :], NT)
            if t == 0:
                gown[:, ks] = total
            else:
                gbuf[t, :, ks] = total.astype(bf16)

        if t:
            send(gbuf.at[t], grecv.at[t], g_s.at[t], g_r.at[t], at_a(for_a))

    for t in range(1, A):
        arrived(ctx_all.at[down_a(t)], x_r.at[t], at_a(down_a(t)))

    ct = tiles_of(C)

    def out_terms(s):
        r = pl.ds(pl.multiple_of(up_m(s) * S, S), S)

        for c in range(C // ct):
            cs = pl.ds(c * ct, ct)
            lhs = ctx_all[:, r, :].reshape(A * S, width)
            for j in range(B):
                term = dot(lhs, w2[j, :, cs]).reshape(A, S, ct)
                if s == 0:
                    oown[j, :, :, cs] = term
                else:
                    obuf[s, j, :, :, cs] = term.astype(bf16)

        if s:
            send(obuf.at[s], orecv.at[s], o_s.at[s], o_r.at[s], at_m(up_m(s)))

    def weight_terms(half, put):
        @pl.loop(0, width // kt)
        def _(i):
            ks = pl.ds(pl.multiple_of(i * kt, kt), kt)
            lhs = ctx_all[:, :, ks].reshape(A * rows, kt)
            rhs = cot_all[half].reshape(A * rows, C)
            put(ks, dot(lhs, rhs, TN))

    for s in range(1, M):
        out_terms(s)

    def put_give(ks, value):
        gwbuf[ks, :] = value.astype(bf16)

    def put_keep(ks, value):
        gw_ref[ks, :] = value

    weight_terms(1 - b, put_give)
    send(gwbuf, gwrecv, h_s.at[0], h_r.at[0], partner)
    out_terms(0)
    weight_terms(b, put_keep)

    for s in range(1, M):
        arrived(orecv.at[s], o_r.at[s], at_m(down_m(s)))

    @pl.loop(0, A)
    def _(i):
        for j in range(B):
            total = oown[j, i]
            for s in range(1, M):
                total = total + orecv[s, j, i].astype(f32)
            summed[j, i] = total.astype(bf16)

    for t in range(1, A):
        send(summed.at[:, up_a(t)], arecv.at[t], z_s.at[t], z_r.at[t], at_a(up_a(t)))
    for j in range(B):
        attn_ref[a, j] = summed[j, a]

    for t in range(1, A):
        arrived(grecv.at[t], g_r.at[t], at_a(down_a(t)))

    @pl.loop(0, heads)
    def _(h):
        cols = pl.ds(pl.multiple_of(h * HEAD_DIM, HEAD_DIM), HEAD_DIM)
        for i in range(rows // PATCHES):
            r = pl.ds(i * PATCHES, PATCHES)
            total = gown[r, cols]
            for t in range(1, A):
                total = total + grecv[t, r, cols].astype(f32)
            dctx = total.astype(bf16)
            q, k = q_ref[r, cols], k_ref[r, cols]
            probs = softmax_of(q, k)
            grad_probs = dot(dctx, v_ref[r, cols], NT)
            inner = jnp.sum(probs * grad_probs, axis=-1, keepdims=True)
            grad_scores = (probs * (grad_probs - inner) * SCALING).astype(bf16)
            gq_ref[r, cols] = dot(grad_scores, k).astype(bf16)
            gk_ref[r, cols] = dot(grad_scores, q, TN).astype(bf16)
            gv_ref[r, cols] = dot(probs.astype(bf16), dctx, TN).astype(bf16)

    arrived(gwrecv, h_r.at[0], partner)

    @pl.loop(0, width // kt)
    def _(i):
        ks = pl.ds(pl.multiple_of(i * kt, kt), kt)
        gw_ref[ks, :] = gw_ref[ks, :] + gwrecv[ks, :].astype(f32)

    for t in range(1, A):
        arrived(arecv.at[t], z_r.at[t], at_a(down_a(t)))
        for j in range(B):
            attn_ref[down_a(t), j] = arecv[t, j]
    for c in sent:
        c.wait_send()


def adam_update(grad_weight, master, moment_one, moment_two):
    new_one = 0.9 * moment_one + 0.1 * grad_weight
    new_two = 0.95 * moment_two + 0.05 * grad_weight * grad_weight
    new_master = master - 0.001 * (new_one / 0.19) / (jnp.sqrt(new_two / 0.0975) + 1e-08)
    return (new_master, new_one, new_two)


def local(queries, keys, values, cotangent, master, moment_one, moment_two):
    bf16, f32 = jnp.bfloat16, jnp.float32
    B = PAIR
    A = lax.axis_size("dp") // B
    M = lax.axis_size("mp")
    rows, width = queries.shape
    S, D = cotangent.shape
    C = master.shape[1]
    cot_blocks = cotangent.reshape(S, A, B, C).transpose(1, 2, 0, 3)
    vmem = pl.BlockSpec(memory_space=pltpu.VMEM)
    dma = pltpu.SemaphoreType.DMA
    act = jax.ShapeDtypeStruct((rows, width), bf16)
    attn, gq, gk, gv, grad_weight = pl.pallas_call(
        functools.partial(main_kernel, A, M),
        in_specs=[vmem] * 5,
        out_specs=[vmem] * 5,
        out_shape=[
            jax.ShapeDtypeStruct((A, B, S, C), bf16), act, act, act,
            jax.ShapeDtypeStruct((width, C), f32),
        ],
        scratch_shapes=[
            pltpu.VMEM((B, width, C), bf16),
            pltpu.VMEM((B, A, M, S, C), bf16),
            pltpu.VMEM((A, rows, width), bf16),
            pltpu.VMEM((A, rows, width), bf16),
            pltpu.VMEM((A, rows, width), bf16),
            pltpu.VMEM((rows, width), f32),
            pltpu.VMEM((M, B, A, S, C), bf16),
            pltpu.VMEM((M, B, A, S, C), bf16),
            pltpu.VMEM((B, A, S, C), f32),
            pltpu.VMEM((B, A, S, C), bf16),
            pltpu.VMEM((A, B, S, C), bf16),
            pltpu.VMEM((width, C), bf16),
            pltpu.VMEM((width, C), bf16),
            dma((1,)), dma((1,)),
            dma((A,)), dma((A,)),
            dma((A, M)), dma((A, M)),
            dma((A,)), dma((A,)),
            dma((A,)), dma((A,)),
            dma((M,)), dma((M,)),
            dma((A,)), dma((A,)),
            dma((1,)), dma((1,)),
        ],
        compiler_params=pltpu.CompilerParams(
            collective_id=0, has_side_effects=True, vmem_limit_bytes=56 * 2**20
        ),
        cost_estimate=pl.CostEstimate(
            flops=6 * A * rows * width * B * C,
            bytes_accessed=16 * rows * width + 8 * width * C,
            transcendentals=2 * rows * PATCHES * width // HEAD_DIM,
        ),
    )(queries, keys, values, cot_blocks, master.astype(bf16))
    attn_out = attn.transpose(2, 0, 1, 3).reshape(S, D)
    news = adam_update(grad_weight, master, moment_one, moment_two)
    return (attn_out, gq, gk, gv, *news)


def solution(mesh):
    in_specs = (
        P("dp", "mp"),
        P("dp", "mp"),
        P("dp", "mp"),
        P(("dp", "mp"), None),
        P("mp", "dp"),
        P("mp", "dp"),
        P("mp", "dp"),
    )
    out_specs = (
        P(("dp", "mp"), None),
        P("dp", "mp"),
        P("dp", "mp"),
        P("dp", "mp"),
        P("mp", "dp"),
        P("mp", "dp"),
        P("mp", "dp"),
    )
    return jax.shard_map(local, mesh=mesh, in_specs=in_specs, out_specs=out_specs, check_vma=False)
```

time: 540 us -> 163 us (0.30)
  waiting for transfers between devices: 433 us -> 0 us
  Pallas kernels: 0 us -> 138 us
  matrix products: 63.6 us -> 0 us
  between operations: 13.9 us -> 0.66 us
  starting transfers between devices: 7.58 us -> 0 us
  local copies, waits for them, and re-layouts: 6.8 us -> 13.9 us
    reduce_scatter x1 -> x0, waiting for transfers between devices: 206 us -> none  [local(): lax.psum_scatter(grad_total.astype(jnp.bfloat16).astype(jnp.float32).asty...]
    all_gather x2 -> x0, waiting for transfers between devices: 200 us -> none  [the longest x1 174 us: local(): lax.all_gather(master.astype(jnp.bfloat16), 'dp', axis=1, tiled=True)]
    pallas_call x0 -> x1, Pallas kernels: none -> 138 us  [local(): pl.pallas_call(functools.partial(main_kernel, A, M), in_specs=[vmem] * 5,...]
    dot_general x11 -> x0, matrix products: 61.5 us -> none  [the longest x4 27.6 us: partial_rows(): return jnp.dot(ctx_rows, columns, preferred_element_type=jnp.float32)]
    ppermute x3 -> x0, waiting for transfers between devices: 26.8 us -> none  [passed_along(): return lax.ppermute(block, axis, route)]
    reshape x1 -> x3, local copies, waits for them, and re-layouts: 1.24 us -> 8.69 us  [the longest x2 5.55 us: local(): cot_blocks = cotangent.reshape(S, A, B, C).transpose(1, 2, 0, 3)]
    ppermute x3 -> x0, starting transfers between devices: 7.28 us -> none  [passed_along(): return lax.ppermute(block, axis, route)]
  transfers between devices with their start and end apart: 6 -> 0, of which waited for: 6 -> 0; matrix products, arithmetic and copies ran while one was open for 1% -> 0% of each run, Pallas kernels for 0% -> 0%
where the time goes in v2:
time: 163 us
  Pallas kernels  138 us (85%)
  local copies, waits for them, and re-layouts  13.9 us (9%)
  other arithmetic  10 us (6%)
    pallas_call x1, Pallas kernels, local(): pl.pallas_call(functools.partial(main_kernel, A, M), in_specs=[vmem] * 5,...  138 us
    sub x1, other arithmetic, adam_update(): master - 0.001 * (new_one / 0.19) / (jnp.sqrt(new_two / 0.0975) + 1e-08)  8.72 us
    reshape x2, local copies, waits for them, and re-layouts, local(): cot_blocks = cotangent.reshape(S, A, B, C).transpose(1, 2, 0, 3)  5.55 us

profile of v2, /device:TPU:19, one launch (start us, length us, event | category | flops | bytes accessed | tf_op | source)
XLA Modules:
  0.0 162.8 jit_solution(5356393508153647709)
XLA Ops:
  0.6 0.0 copy-start
  0.6 3.4 %reshape.20 = bf16[64,4,2,768]{3,2,1,0:T(2,128)(2,1)} reshape(bf16[64,6144]{1,0:T(8,128)(2,1)} %param.10) | data formatting | bytes 1572864 | tf_op jit(solution)/shard_map/reshape | solution.py:253
  4.0 2.1 %copy.17 = bf16[64,4,2,768]{3,0,2,1:T(8,128)(2,1)} copy(bf16[64,4,2,768]{3,2,1,0:T(2,128)(2,1)} %reshape.20) | data formatting | bytes 1572864 | tf_op jit(solution)/shard_map/reshape | solution.py:253
  6.2 0.0 copy-done
  6.2 1.3 convert_element_type.3.wb
  7.5 138.2 %shard_map.126 = (bf16[4,2,64,768]{3,2,1,0:T(8,128)(2,1)}, bf16[256,1024]{1,0:T(8,128)(2,1)}, bf16[256,1024]{1,0:T(8,128)(2,1)}, bf16[256,1024]{1,0:T(8,128)(2,1)}, f32[1024,768]{1,0:T(8,128)}) custom-call(bf16[256,1024]{1,0:T(8,128)(2,1)} %q_ref.1, bf16[256,1024]{1,0:T(8,128)(2,1)} %k_ref.1, bf16[256,1024]{1,0:T(8,128)(2,1)} %v_ref.1, ...), custom_call_target="tpu_custom_call" | custom-call | flops 9663676416 | bytes 10485760 | tf_op jit(solution)/shard_map/pallas_call | solution.py:257
  145.7 2.8 %copy.15 = bf16[64,4,2,768]{3,2,1,0:T(2,128)(2,1)} copy(bf16[64,4,2,768]{3,0,2,1:T(8,128)(2,1)} %bitcast.5) | data formatting | bytes 1572864 | tf_op jit(solution)/shard_map/transpose | solution.py:297
  148.5 3.1 %reshape.21 = bf16[64,6144]{1,0:T(8,128)(2,1)} reshape(bf16[64,4,2,768]{3,2,1,0:T(2,128)(2,1)} %copy.15) | data formatting | bytes 1572864 | tf_op jit(solution)/shard_map/reshape | solution.py:297
  151.7 0.0 copy-start.3
  151.7 0.0 copy-start.2
  151.7 0.0 copy-start.1
  151.7 8.7 %divide_subtract_fusion = (f32[1024,768]{1,0:T(8,128)}, f32[1024,768]{1,0:T(8,128)}, f32[1024,768]{1,0:T(8,128)}) fusion(f32[1024,768]{1,0:T(8,128)S(1)} %copy-done, f32[1024,768]{1,0:T(8,128)} %get-tuple-element.16, f32[1024,768]{1,0:T(8,128)} %param.12, f32[1024,768]{1,0:T(8,128)} %param.13), kind=kLoop, calls=%fused_computation.2 | loop fusion | flops 9437184 | bytes 22020096 | tf_op jit(solution)/shard_map/sub | solution.py:241
  160.4 0.0 copy-done.3
  160.4 0.8 copy.21
  161.2 0.0 copy-done.2
  161.2 0.8 copy.22
  162.0 0.0 copy-done.1
  162.0 0.8 copy.23
Async XLA Ops:
  0.6 5.6 %copy-start = (f32[1024,768]{1,0:T(8,128)S(1)}, f32[1024,768]{1,0:T(8,128)}, u32[]{:S(2)}) copy-start(f32[1024,768]{1,0:T(8,128)} %param.11) | copy-start | bytes 9437188
  151.7 8.7 %copy-start.3 = (bf16[256,1024]{1,0:T(8,128)(2,1)S(1)}, bf16[256,1024]{1,0:T(8,128)(2,1)}, u32[]{:S(2)}) copy-start(bf16[256,1024]{1,0:T(8,128)(2,1)} %get-tuple-element.28) | copy-start | bytes 1572868
  151.7 9.5 %copy-start.2 = (bf16[256,1024]{1,0:T(8,128)(2,1)S(1)}, bf16[256,1024]{1,0:T(8,128)(2,1)}, u32[]{:S(2)}) copy-start(bf16[256,1024]{1,0:T(8,128)(2,1)} %get-tuple-element.29) | copy-start | bytes 1572868
  151.7 10.3 %copy-start.1 = (bf16[256,1024]{1,0:T(8,128)(2,1)S(1)}, bf16[256,1024]{1,0:T(8,128)(2,1)}, u32[]{:S(2)}) copy-start(bf16[256,1024]{1,0:T(8,128)(2,1)} %get-tuple-element.30) | copy-start | bytes 1572868

commit v3 on v2

--- a/solution.py
+++ b/solution.py
@@ -43,7 +43,9 @@
     d, m = lax.axis_index("dp"), lax.axis_index("mp")
     a, b = d // B, d % B
     rows, width = q_ref.shape
-    S, C = cotb.shape[2:]
+    C = wb.shape[1]
+    direct = C % HEAD_DIM == 0
+    S = cotb.shape[0] if direct else cotb.shape[2]
     heads = width // HEAD_DIM
 
     def at_a(i):
@@ -72,6 +74,9 @@
             device_id=device, device_id_type=MESH,
         )
 
+    def columns(i, j):
+        return pl.ds(pl.multiple_of((i * B + j) * C, HEAD_DIM), C)
+
     barrier = pltpu.get_barrier_semaphore()
     peers = [at_a(up_a(t)) for t in range(1, A)] + [at_m(up_m(s)) for s in range(1, M)] + [partner]
     for peer in peers:
@@ -90,10 +95,12 @@
 
     for t in range(1, A):
         to = up_a(t)
-        send(cotb.at[to], cot_all.at[:, a, m], cz_s.at[t], cz_r.at[t], at_a(to))
+        for j in range(B):
+            block = cotb.at[:, columns(to, j)] if direct else cotb.at[to, j]
+            send(block, cot_all.at[j, a, m], cz_s.at[t, j], cz_r.at[t, j], at_a(to))
     send(wb, w2.at[b], w_s.at[0], w_r.at[0], partner)
     for j in range(B):
-        cot_all[j, a, m] = cotb[a, j]
+        cot_all[j, a, m] = cotb[:, columns(a, j)] if direct else cotb[a, j]
     w2[b] = wb[...]
 
     def spread(t):
@@ -113,10 +120,38 @@
             ctx_all[a, r, cols] = dot(probs, v_ref[r, cols]).astype(bf16)
 
     for t in range(1, A):
-        arrived(cot_all.at[:, down_a(t), m], cz_r.at[t], at_a(down_a(t)))
+        for j in range(B):
+            arrived(cot_all.at[j, down_a(t), m], cz_r.at[t, j], at_a(down_a(t)))
         spread(t)
-    for t in range(1, A):
-        send(ctx_all.at[a], ctx_all.at[a], x_s.at[t], x_r.at[t], at_a(up_a(t)))
+
+    def hop(way, k):
+        block = ctx_all.at[a - k if way == 0 else a + k]
+        to = a + 1 if way == 0 else a - 1
+        origin = a - k if way == 0 else a + k
+        return copy(block, block, x_s.at[way, k], x_r.at[origin], at_a(to))
+
+    def passes(way, k):
+        if way == 0:
+            return (a >= k) & (a + 1 < A)
+        return (a + k < A) & (a >= 1)
+
+    def take(way, k):
+        origin = a - k if way == 0 else a + k
+
+        @pl.when(a >= k if way == 0 else a + k < A)
+        def _():
+            arrived(ctx_all.at[origin], x_r.at[origin], at_a(a - 1 if way == 0 else a + 1))
+
+    def pass_on(way, k):
+        @pl.when(passes(way, k))
+        def _():
+            hop(way, k).start()
+
+    for k in range(A - 1):
+        for way in range(2):
+            if k:
+                take(way, k)
+            pass_on(way, k)
 
     arrived(w2.at[1 - b], w_r.at[0], partner)
     kt = tiles_of(width)
@@ -140,8 +175,9 @@
         if t:
             send(gbuf.at[t], grecv.at[t], g_s.at[t], g_r.at[t], at_a(for_a))
 
-    for t in range(1, A):
-        arrived(ctx_all.at[down_a(t)], x_r.at[t], at_a(down_a(t)))
+    for way in range(2):
+        if A > 1:
+            take(way, A - 1)
 
     ct = tiles_of(C)
 
@@ -196,8 +232,15 @@
 
     for t in range(1, A):
         send(summed.at[:, up_a(t)], arecv.at[t], z_s.at[t], z_r.at[t], at_a(up_a(t)))
+
+    def put_attn(i, j, value):
+        if direct:
+            attn_ref[:, columns(i, j)] = value
+        else:
+            attn_ref[i, j] = value
+
     for j in range(B):
-        attn_ref[a, j] = summed[j, a]
+        put_attn(a, j, summed[j, a])
 
     for t in range(1, A):
         arrived(grecv.at[t], g_r.at[t], at_a(down_a(t)))
@@ -230,9 +273,15 @@
     for t in range(1, A):
         arrived(arecv.at[t], z_r.at[t], at_a(down_a(t)))
         for j in range(B):
-            attn_ref[down_a(t), j] = arecv[t, j]
+            put_attn(down_a(t), j, arecv[t, j])
     for c in sent:
         c.wait_send()
+    for k in range(A - 1):
+        for way in range(2):
+
+            @pl.when(passes(way, k))
+            def _():
+                hop(way, k).wait_send()
 
 
 def adam_update(grad_weight, master, moment_one, moment_two):
@@ -250,7 +299,11 @@
     rows, width = queries.shape
     S, D = cotangent.shape
     C = master.shape[1]
-    cot_blocks = cotangent.reshape(S, A, B, C).transpose(1, 2, 0, 3)
+    direct = C % HEAD_DIM == 0
+    if direct:
+        cot_blocks = cotangent
+    else:
+        cot_blocks = cotangent.reshape(S, A, B, C).transpose(1, 2, 0, 3)
     vmem = pl.BlockSpec(memory_space=pltpu.VMEM)
     dma = pltpu.SemaphoreType.DMA
     act = jax.ShapeDtypeStruct((rows, width), bf16)
@@ -259,7 +312,7 @@
         in_specs=[vmem] * 5,
         out_specs=[vmem] * 5,
         out_shape=[
-            jax.ShapeDtypeStruct((A, B, S, C), bf16), act, act, act,
+            jax.ShapeDtypeStruct((S, D) if direct else (A, B, S, C), bf16), act, act, act,
             jax.ShapeDtypeStruct((width, C), f32),
         ],
         scratch_shapes=[
@@ -277,9 +330,9 @@
             pltpu.VMEM((width, C), bf16),
             pltpu.VMEM((width, C), bf16),
             dma((1,)), dma((1,)),
-            dma((A,)), dma((A,)),
+            dma((A, B)), dma((A, B)),
             dma((A, M)), dma((A, M)),
-            dma((A,)), dma((A,)),
+            dma((2, A)), dma((A,)),
             dma((A,)), dma((A,)),
             dma((M,)), dma((M,)),
             dma((A,)), dma((A,)),
@@ -294,7 +347,7 @@
             transcendentals=2 * rows * PATCHES * width // HEAD_DIM,
         ),
     )(queries, keys, values, cot_blocks, master.astype(bf16))
-    attn_out = attn.transpose(2, 0, 1, 3).reshape(S, D)
+    attn_out = attn if direct else attn.transpose(2, 0, 1, 3).reshape(S, D)
     news = adam_update(grad_weight, master, moment_one, moment_two)
     return (attn_out, gq, gk, gv, *news)
 

time: 163 us -> 135 us (0.83); the launches traced: 163 us -> 132 us
  Pallas kernels: 138 us -> 117 us
  local copies, waits for them, and re-layouts: 13.9 us -> 3.28 us
    pallas_call x1, Pallas kernels: 138 us -> 117 us  [local(): pl.pallas_call(functools.partial(main_kernel, A, M), in_specs=[vmem] * 5,...]
    reshape x3 -> x0, local copies, waits for them, and re-layouts: 8.69 us -> none  [the longest x2 5.55 us: local(): cot_blocks = cotangent.reshape(S, A, B, C).transpose(1, 2, 0, 3)]
    transpose x1 -> x0, local copies, waits for them, and re-layouts: 2.82 us -> none  [local(): attn_out = attn.transpose(2, 0, 1, 3).reshape(S, D)]
    convert_element_type x1, other arithmetic: 1.3 us -> 3.19 us  [local(): master.astype(bf16)]
    unnamed x11 -> x16, local copies, waits for them, and re-layouts: 2.39 us -> 3.28 us
where the time goes in v3:
time: 135 us; the launch traced here: 132 us
  Pallas kernels  117 us (87%)
  other arithmetic  11 us (8%)
  local copies, waits for them, and re-layouts  3.28 us (2%)
    pallas_call x1, Pallas kernels, local(): pl.pallas_call(functools.partial(main_kernel, A, M), in_specs=[vmem] * 5,...  117 us
    sub x1, other arithmetic, adam_update(): master - 0.001 * (new_one / 0.19) / (jnp.sqrt(new_two / 0.0975) + 1e-08)  7.83 us
    unnamed x16, local copies, waits for them, and re-layouts  3.28 us
    convert_element_type x1, other arithmetic, local(): master.astype(bf16)  3.19 us

profile of v3, /device:TPU:19, one launch (start us, length us, event | category | flops | bytes accessed | tf_op | source)
XLA Modules:
  0.0 132.3 jit_solution(5988087622503024586)
XLA Ops:
  0.6 3.2 %convert_element_type.3.wb = bf16[1024,768]{1,0:T(8,128)(2,1)} convert(f32[1024,768]{1,0:T(8,128)} %param.11) | non-fusion elementwise | flops 786432 | bytes 4718592 | tf_op jit(solution)/shard_map/convert_element_type | solution.py:349
  3.8 0.0 copy-start
  3.8 0.0 copy-start.1
  3.8 117.3 %shard_map.126 = (bf16[64,6144]{1,0:T(8,128)(2,1)}, bf16[256,1024]{1,0:T(8,128)(2,1)}, bf16[256,1024]{1,0:T(8,128)(2,1)}, bf16[256,1024]{1,0:T(8,128)(2,1)}, f32[1024,768]{1,0:T(8,128)}) custom-call(bf16[256,1024]{1,0:T(8,128)(2,1)} %q_ref.1, bf16[256,1024]{1,0:T(8,128)(2,1)} %k_ref.1, bf16[256,1024]{1,0:T(8,128)(2,1)} %v_ref.1, bf16[64,6144]{1,0:T(8,128)(2,1)} %cotb.1, ...), custom_call_target="tpu_custom_call" | custom-call | flops 9663676416 | bytes 10485760 | tf_op jit(solution)/shard_map/pallas_call | solution.py:310
  121.2 0.0 copy-done
  121.2 0.0 copy-done.1
  121.2 0.0 copy-start.2
  121.2 0.0 copy-start.5
  121.2 0.0 copy-start.4
  121.2 7.8 %divide_subtract_fusion = (f32[1024,768]{1,0:T(8,128)}, f32[1024,768]{1,0:T(8,128)}, f32[1024,768]{1,0:T(8,128)}) fusion(f32[1024,768]{1,0:T(8,128)S(1)} %copy-done, f32[1024,768]{1,0:T(8,128)} %get-tuple-element.16, f32[1024,768]{1,0:T(8,128)S(1)} %copy-done.1, f32[1024,768]{1,0:T(8,128)} %param.13), kind=kLoop, calls=%fused_computation.2 | loop fusion | flops 9437184 | bytes 22020096 | tf_op jit(solution)/shard_map/sub | solution.py:290
  129.1 0.0 copy-start.3
  129.1 0.0 copy-done.2
  129.1 0.9 copy.18
  129.9 0.0 copy-done.5
  129.9 0.8 copy.19
  130.7 0.0 copy-done.4
  130.7 0.8 copy.20
  131.5 0.0 copy-done.3
  131.5 0.8 copy.21
Async XLA Ops:
  3.8 117.4 %copy-start = (f32[1024,768]{1,0:T(8,128)S(1)}, f32[1024,768]{1,0:T(8,128)}, u32[]{:S(2)}) copy-start(f32[1024,768]{1,0:T(8,128)} %param.11) | copy-start | bytes 9437188
  3.8 117.4 %copy-start.1 = (f32[1024,768]{1,0:T(8,128)S(1)}, f32[1024,768]{1,0:T(8,128)}, u32[]{:S(2)}) copy-start(f32[1024,768]{1,0:T(8,128)} %param.12) | copy-start | bytes 9437188
  121.2 7.9 %copy-start.2 = (bf16[64,6144]{1,0:T(8,128)(2,1)S(1)}, bf16[64,6144]{1,0:T(8,128)(2,1)}, u32[]{:S(2)}) copy-start(bf16[64,6144]{1,0:T(8,128)(2,1)} %get-tuple-element.27) | copy-start | bytes 2359300
  121.2 8.7 %copy-start.5 = (bf16[256,1024]{1,0:T(8,128)(2,1)S(1)}, bf16[256,1024]{1,0:T(8,128)(2,1)}, u32[]{:S(2)}) copy-start(bf16[256,1024]{1,0:T(8,128)(2,1)} %get-tuple-element.28) | copy-start | bytes 1572868
  121.2 9.5 %copy-start.4 = (bf16[256,1024]{1,0:T(8,128)(2,1)S(1)}, bf16[256,1024]{1,0:T(8,128)(2,1)}, u32[]{:S(2)}) copy-start(bf16[256,1024]{1,0:T(8,128)(2,1)} %get-tuple-element.29) | copy-start | bytes 1572868
  129.1 2.5 %copy-start.3 = (bf16[256,1024]{1,0:T(8,128)(2,1)S(1)}, bf16[256,1024]{1,0:T(8,128)(2,1)}, u32[]{:S(2)}) copy-start(bf16[256,1024]{1,0:T(8,128)(2,1)} %get-tuple-element.30) | copy-start | bytes 1572868
